TPU v7x, 32 devices: a whole 2x2x4 slice. The times are simulated.
32 devices in a mesh: dp: 8 (over y, x, core), tensor: 4 (over z).
Axes of the slice: x: 2, y: 2, z: 4, core: 2. Of those that a mesh axis runs over, the one named last changes fastest.
Arguments:
- hidden: bfloat16 [64, 16384], P('dp'), may hold values from -6 to 6
- norm_gain: bfloat16 [16384], replicated, may hold values from 0.099609375 to 1.8984375
- query_weight: bfloat16 [16384, 16384], P('dp', 'tensor'), may hold values from -0.046875 to 0.046875
- keyval_weight: bfloat16 [16384, 8, 256], P('dp', 'tensor'), may hold values from -0.046875 to 0.046875
- output_weight: bfloat16 [16384, 16384], P('tensor', 'dp'), may hold values from -0.046875 to 0.046875
- kv_cache: bfloat16 [64, 8, 1024, 256], P('dp', 'tensor')
- cache_lengths: int32 [64], P('dp'), may hold values from 128 to 1024, as said below
- next_source: bfloat16 [128, 128, 16384], P(('dp', 'tensor')), may hold values from -0.046875 to 0.046875
- block_ids: int32 [128], P('dp'), may hold values from 0 to 127, as said below
Outputs:
- mixed: bfloat16 [64, 16384], P('dp')
- next_weight: bfloat16 [16384, 16384], P('dp', 'tensor')
Inputs may be any that keep to these rules, and one draw needn't show every extreme that they name: `cache_lengths`: some row uses exactly 1024 positions. `block_ids`: a permutation; the 16 entries on one dp index name at most 2 blocks within the rows of any one dp index, and that many for some.
All inputs are finite; a program needn't handle non-finite values.
Results may differ from a plain program's by a relative error of at most 0.04.
Values may be sent and summed in bfloat16 or wider, within the bound.
A program may use at most 192 MiB of HBM per device.

v0:
```python
import jax
import jax.numpy as jnp
from jax import lax
from jax.sharding import PartitionSpec as P


def attend(queries, new_keyval, kv_cache, cache_lengths):
    rows, groups, length, twice = kv_cache.shape
    head_dim = twice // 2
    score_scale = head_dim ** (-0.5)
    query_heads = queries.reshape(rows, groups, -1, head_dim)
    scores = (
        jnp.einsum(
            "rjhd,rjpd->rjhp",
            query_heads,
            kv_cache[..., :head_dim],
            preferred_element_type=jnp.float32,
        )
        * score_scale
    )
    visible = jnp.arange(length)[None, :] < cache_lengths[:, None]
    scores = jnp.where(visible[:, None, None, :], scores, -jnp.inf)
    self_score = (
        jnp.einsum(
            "rjhd,rjd->rjh",
            query_heads,
            new_keyval[..., :head_dim],
            preferred_element_type=jnp.float32,
        )
        * score_scale
    )
    highest = jnp.maximum(jnp.max(scores, axis=-1), self_score)
    expo = jnp.exp(scores - highest[..., None])
    self_expo = jnp.exp(self_score - highest)
    denominator = jnp.sum(expo, axis=-1) + self_expo
    weights = (expo / denominator[..., None]).astype(jnp.bfloat16)
    self_weight = (self_expo / denominator).astype(jnp.bfloat16)
    summed = jnp.einsum(
        "rjhp,rjpd->rjhd", weights, kv_cache[..., head_dim:], preferred_element_type=jnp.float32
    )
    summed = summed + self_weight.astype(jnp.float32)[..., None] * new_keyval[
        :, :, None, head_dim:
    ].astype(jnp.float32)
    return summed.astype(jnp.bfloat16).reshape(rows, -1)


def relayout(next_source, block_ids):
    dp_count = lax.axis_size("dp")
    columns = lax.all_to_all(next_source, "tensor", split_axis=2, concat_axis=0, tiled=True)
    group_size = columns.shape[0]
    capacity = max(1, group_size // dp_count)
    mine_dp = lax.axis_index("dp")
    target = block_ids // group_size
    onehot = (target[:, None] == jnp.arange(dp_count, dtype=jnp.int32)[None, :]).astype(jnp.int32)
    arrival = jnp.sum((jnp.cumsum(onehot, axis=0) - onehot) * onehot, axis=1)
    slot_index = target * capacity + arrival
    select = jnp.arange(dp_count * capacity, dtype=jnp.int32)[:, None] == slot_index[None, :]
    outgoing = jnp.einsum(
        "sb,brc->src", select.astype(jnp.bfloat16), columns, preferred_element_type=jnp.float32
    ).astype(jnp.bfloat16)
    outgoing_ids = jnp.sum(jnp.where(select, block_ids[None, :] + 1, 0), axis=1) - 1
    incoming, incoming_ids = (
        lax.all_to_all(outgoing, "dp", split_axis=0, concat_axis=0, tiled=True),
        lax.all_to_all(outgoing_ids, "dp", split_axis=0, concat_axis=0, tiled=True),
    )
    position = incoming_ids - mine_dp * group_size
    place_table = (jnp.arange(group_size, dtype=jnp.int32)[:, None] == position[None, :]).astype(
        jnp.bfloat16
    )
    placed = jnp.einsum(
        "gs,src->grc", place_table, incoming, preferred_element_type=jnp.float32
    ).astype(jnp.bfloat16)
    return placed.reshape(group_size * placed.shape[1], placed.shape[2])


def on_device(
    hidden,
    norm_gain,
    query_weight,
    keyval_weight,
    output_weight,
    kv_cache,
    cache_lengths,
    next_source,
    block_ids,
):
    rows_dev = hidden.shape[0]
    stream = hidden.astype(jnp.float32)
    meansq = jnp.mean(stream * stream, axis=-1, keepdims=True)
    normed = (stream * lax.rsqrt(meansq + 1e-05) * norm_gain.astype(jnp.float32)).astype(
        jnp.bfloat16
    )
    pieces = lax.all_to_all(normed, "dp", split_axis=1, concat_axis=0, tiled=True)
    flat_kv = keyval_weight.reshape(keyval_weight.shape[0], -1)
    query_cols = query_weight.shape[1]
    projected = lax.psum_scatter(
        jnp.concatenate(
            [
                jnp.dot(pieces, query_weight, preferred_element_type=jnp.float32),
                jnp.dot(pieces, flat_kv, preferred_element_type=jnp.float32),
            ],
            axis=1,
        ).astype(jnp.bfloat16),
        "dp",
        scatter_dimension=0,
        tiled=True,
    ).astype(jnp.float32)
    queries = projected[:, :query_cols].astype(jnp.bfloat16)
    new_keyval = (
        projected[:, query_cols:]
        .astype(jnp.bfloat16)
        .reshape(rows_dev, keyval_weight.shape[1], keyval_weight.shape[2])
    )
    heads_out = attend(queries, new_keyval, kv_cache, cache_lengths)
    next_weight = relayout(next_source, block_ids)
    partial_out = jnp.dot(
        lax.all_gather(heads_out, "dp", axis=0, tiled=True),
        output_weight,
        preferred_element_type=jnp.float32,
    )
    summed = lax.psum(partial_out.astype(jnp.bfloat16), "tensor")
    attention = lax.all_to_all(summed, "dp", split_axis=0, concat_axis=1, tiled=True)
    mixed = (stream + attention.astype(jnp.float32)).astype(jnp.bfloat16)
    return (mixed, next_weight)


def solution(mesh):
    return jax.shard_map(
        on_device,
        mesh=mesh,
        in_specs=(
            P("dp", None),
            P(),
            P("dp", "tensor"),
            P("dp", "tensor", None),
            P("tensor", "dp"),
            P("dp", "tensor", None, None),
            P("dp"),
            P(("dp", "tensor"), None, None),
            P("dp"),
        ),
        out_specs=(P("dp", None), P("dp", "tensor")),
        check_vma=False,
    )
```

profile of v0, /device:TPU:0, one launch (start us, length us, event | category | flops | bytes accessed | tf_op | source)
XLA Modules:
  0.0 768.0 jit_solution(16237021047967786808)
XLA Ops:
  7.2 1.2 fusion.28
  9.1 1.8 fusion.30
  10.9 5.2 all-to-all-start
  16.1 26.0 %copy.25 = bf16[4,128,16384]{1,0,2:T(4,128)(2,1)} copy(bf16[4,128,16384]{2,1,0:T(8,128)(2,1)} %param.16) | data formatting | bytes 33554432 | tf_op args[7]
  42.1 7.1 all-to-all-start.3
  50.2 8.8 %convolution_convert_fusion = bf16[64,4096]{1,0:T(8,128)(2,1)S(1)} fusion(bf16[2048,4096]{1,0:T(8,128)(2,1)} %param.11, bf16[8,8,2048]{2,0,1:T(8,128)(2,1)S(1)} %all-to-all-done), kind=kOutput, calls=%fused_computation.6 | convolution fusion | flops 1074003968 | bytes 17563648 | tf_op jit(solution)/shard_map/dot_general | solution.py:99
  59.0 0.8 pad_maximum_fusion
  60.3 36.0 %reduce-scatter.2.cloned.1.call-done = bf16[8,4608]{1,0:T(8,128)(2,1)} async-done(((bf16[64,4608]{1,0:T(8,128)(2,1)}), bf16[8,4608]{1,0:T(8,128)(2,1)}) %reduce-scatter.2.cloned.1.call-update) | async-done | bytes 73744 | tf_op jit(solution)/shard_map/reduce_scatter | solution.py:96
  97.0 0.8 slice.26
  98.0 3.5 fusion.49
  101.8 3.0 fusion.24
  104.9 9.8 %all_gather.3 = bf16[64,4096]{1,0:T(8,128)(2,1)S(1)} all-gather(bf16[8,4096]{1,0:T(8,128)(2,1)S(1)} %bitcast.48), channel_id=1, replica_groups=mesh['dp'=8,'tensor'=4] {'dp'}, dimensions={0}, use_global_device_ids=true | all-gather | bytes 589824 | tf_op jit(solution)/shard_map/all_gather | solution.py:117
  114.6 9.5 %fusion.14 = bf16[8,8,2048]{2,1,0:T(8,128)(2,1)} fusion(bf16[64,4096]{1,0:T(8,128)(2,1)S(1)} %all_gather.3, bf16[4096,2048]{1,0:T(8,128)(2,1)} %param.13), kind=kOutput, calls=%fused_computation.12 | convolution fusion | flops 1073872896 | bytes 17563648 | tf_op jit(solution)/shard_map/dot_general | solution.py:116
  125.0 296.4 %all-to-all-done.3 = bf16[4,128,16384]{1,0,2:T(4,128)(2,1)} async-done(((bf16[4,128,16384]{1,0,2:T(4,128)(2,1)}), bf16[4,128,16384]{1,0,2:T(4,128)(2,1)}, u32[]{:S(2)}, u32[]{:S(2)}) %all-to-all-start.3) | async-done | bytes 16777248 | tf_op jit(solution)/shard_map/all_to_all | solution.py:49
  421.4 3.8 all-to-all-start.2
  425.2 15.1 %copy.26 = bf16[4,128,16384]{1,2,0:T(8,128)(2,1)} copy(bf16[4,128,16384]{1,0,2:T(4,128)(2,1)} %all-to-all-done.3) | data formatting | bytes 33554432 | tf_op jit(solution)/shard_map/all_to_all | solution.py:49
  440.4 20.8 %copy.27 = bf16[4,4,128,4096]{3,2,1,0:T(8,128)(2,1)} copy(bf16[4,4,128,4096]{2,3,0,1:T(8,128)(2,1)} %bitcast.43) | data formatting | bytes 33554432 | tf_op jit(solution)/shard_map/all_to_all | solution.py:49
  461.2 4.5 all-to-all-start.1
  465.7 29.5 %fusion.4 = bf16[16,128,4096]{2,0,1:T(8,128)(2,1)} fusion(bf16[16,128,4096]{2,1,0:T(8,128)(2,1)} %bitcast.42, s32[16]{0:T(128)S(1)} %multiply_add_fusion), kind=kOutput, calls=%fused_computation.4 | convolution fusion | flops 276824320 | bytes 33554496 | tf_op jit(solution)/shard_map/sb,brc->src/dot_general | solution.py:58
  495.3 18.5 %copy.29 = bf16[16,128,4096]{2,1,0:T(8,128)(2,1)} copy(bf16[16,128,4096]{2,0,1:T(8,128)(2,1)} %fusion.4) | data formatting | bytes 33554432 | tf_op jit(solution)/shard_map/convert_element_type | solution.py:60
  513.8 5.9 all-to-all-start.4
  520.6 183.0 %all-to-all-done.4 = bf16[16,128,4096]{2,1,0:T(8,128)(2,1)} async-done(((bf16[16,128,4096]{2,1,0:T(8,128)(2,1)}), bf16[16,128,4096]{2,1,0:T(8,128)(2,1)}, u32[]{:S(2)}, u32[]{:S(2)}) %all-to-all-start.4) | async-done | bytes 16777248 | tf_op jit(solution)/shard_map/all_to_all | solution.py:63
  703.6 38.9 %fusion.7 = bf16[16,128,4096]{2,0,1:T(8,128)(2,1)} fusion(bf16[16,128,4096]{2,1,0:T(8,128)(2,1)} %all-to-all-done.4, s32[16]{0:T(128)S(1)} %sub.45), kind=kOutput, calls=%fused_computation.5 | convolution fusion | flops 276824320 | bytes 33554496 | tf_op jit(solution)/shard_map/gs,src->grc/dot_general | solution.py:70
  742.5 18.5 %copy.31 = bf16[16,128,4096]{2,1,0:T(8,128)(2,1)} copy(bf16[16,128,4096]{2,0,1:T(8,128)(2,1)} %fusion.7) | data formatting | bytes 33554432 | tf_op jit(solution)/shard_map/convert_element_type | solution.py:72
  (41 shorter events, 5.2 us)
Async XLA Ops:
  10.9 31.1 %all-to-all-start = ((bf16[8,8,2048]{2,0,1:T(8,128)(2,1)}), bf16[8,8,2048]{2,0,1:T(8,128)(2,1)S(1)}, u32[]{:S(2)}, u32[]{:S(2)}) async-start(bf16[8,8,2048]{2,0,1:T(8,128)(2,1)} %bitcast), calls=%async_computation | async-start | bytes 524288 | tf_op jit(solution)/shard_map/all_to_all | solution.py:93
  42.1 7.2 copy-start.1
  42.1 379.3 %all-to-all-start.3 = ((bf16[4,128,16384]{1,0,2:T(4,128)(2,1)}), bf16[4,128,16384]{1,0,2:T(4,128)(2,1)}, u32[]{:S(2)}, u32[]{:S(2)}) async-start(bf16[4,128,16384]{1,0,2:T(4,128)(2,1)} %copy.25), calls=%async_computation.4 | async-start | bytes 33554432 | tf_op jit(solution)/shard_map/all_to_all | solution.py:49
  49.2 10.7 %copy-start.3 = (s32[16]{0:T(128)S(1)}, s32[16]{0:T(128)}, u32[]{:S(2)}) copy-start(s32[16]{0:T(128)} %param.17) | copy-start | bytes 196
  49.2 11.1 %copy-start.2 = (s32[8]{0:T(128)S(1)}, s32[8]{0:T(128)}, u32[]{:S(2)}) copy-start(s32[8]{0:T(128)} %param.15) | copy-start | bytes 100
  49.2 47.1 %reduce-scatter.2.cloned.1.call-start = ((), (), s32[]{:S(2)}) async-start(), calls=%async_computation.6 | async-start | bytes 663552 | tf_op jit(solution)/shard_map/reduce_scatter | solution.py:96
  59.9 401.4 %all-reduce.2.cloned.1.call-start = ((), (), s32[]{:S(2)}) async-start(), calls=%async_computation.7 | async-start | bytes 524288 | tf_op jit(solution)/shard_map/psum | solution.py:121
  421.4 39.8 %all-to-all-start.2 = ((s32[8,2,1]{1,2,0:T(1,128)}), s32[8,2,1]{1,2,0:T(1,128)S(1)}, u32[]{:S(2)}, u32[]{:S(2)}) async-start(s32[8,2,1]{1,2,0:T(1,128)} %bitcast.12), calls=%async_computation.3 | async-start | bytes 8192 | tf_op jit(solution)/shard_map/all_to_all | solution.py:64
  461.2 52.5 %all-to-all-start.1 = ((bf16[8,8,2048]{2,1,0:T(8,128)(2,1)}), bf16[8,8,2048]{2,1,0:T(8,128)(2,1)S(1)}, u32[]{:S(2)}, u32[]{:S(2)}) async-start(bf16[8,8,2048]{2,1,0:T(8,128)(2,1)} %all-reduce.2.cloned.1.call-done), calls=%async_computation.2 | async-start | bytes 524288 | tf_op jit(solution)/shard_map/all_to_all | solution.py:122
  513.8 6.1 copy-start
  513.8 189.8 %all-to-all-start.4 = ((bf16[16,128,4096]{2,1,0:T(8,128)(2,1)}), bf16[16,128,4096]{2,1,0:T(8,128)(2,1)}, u32[]{:S(2)}, u32[]{:S(2)}) async-start(bf16[16,128,4096]{2,1,0:T(8,128)(2,1)} %copy.29), calls=%async_computation.5 | async-start | bytes 33554432 | tf_op jit(solution)/shard_map/all_to_all | solution.py:63
Sparse Core Ops, SparseCore 0:
  60.0 36.2 reduce-scatter.1
  124.3 53.8 all-reduce.1
where the time goes:
time: 778 us; the launch traced here: 768 us
  waiting for transfers between devices  515 us (66%)
  local copies, waits for them, and re-layouts  102 us (13%)
  matrix products  93.8 us (12%)
  starting transfers between devices  26.6 us (3%)
  between operations  14.4 us (2%)
  blocking collectives  9.78 us (1%)
    all_to_all x1, waiting for transfers between devices, relayout(): lax.all_to_all(next_source, 'tensor', split_axis=2, concat_axis=0, tiled=...  296 us
    all_to_all x1, waiting for transfers between devices, relayout(): lax.all_to_all(outgoing, 'dp', split_axis=0, concat_axis=0, tiled=True)  183 us
    dot_general x1, matrix products, relayout(): jnp.einsum('gs,src->grc', place_table, incoming, preferred_element_type=j...  38.9 us
    all_to_all x2, local copies, waits for them, and re-layouts, relayout(): lax.all_to_all(next_source, 'tensor', split_axis=2, concat_axis=0, tiled=...  36 us
    reduce_scatter x1, waiting for transfers between devices, on_device(): lax.psum_scatter(jnp.concatenate([jnp.dot(pieces, query_weight, preferred...  36 us
    dot_general x1, matrix products, relayout(): jnp.einsum('sb,brc->src', select.astype(jnp.bfloat16), columns, preferred...  29.5 us
    unnamed x11, local copies, waits for them, and re-layouts  26.5 us
    convert_element_type x1, local copies, waits for them, and re-layouts, relayout(): placed = jnp.einsum('gs,src->grc', place_table, incoming, preferred_eleme...  18.5 us
  transfers between devices with their start and end apart: 7, of which 3 were waited for; matrix products, arithmetic and copies ran while one was open for 18% of the time, Pallas kernels for 0%

commit v1 on v0

--- a/solution.py
+++ b/solution.py
@@ -1,6 +1,10 @@
+import functools
+
 import jax
 import jax.numpy as jnp
 from jax import lax
+from jax.experimental import pallas as pl
+from jax.experimental.pallas import tpu as pltpu
 from jax.sharding import PartitionSpec as P
 
 
@@ -44,33 +48,252 @@
     return summed.astype(jnp.bfloat16).reshape(rows, -1)
 
 
-def relayout(next_source, block_ids):
-    dp_count = lax.axis_size("dp")
-    columns = lax.all_to_all(next_source, "tensor", split_axis=2, concat_axis=0, tiled=True)
-    group_size = columns.shape[0]
+CHUNK = 16
+EARLY = 48
+AHEAD = 3
+
+
+def route_kernel(
+    dp_count,
+    tensor_count,
+    early_chunks,
+    send_index,
+    source,
+    early,
+    summed,
+    incoming,
+    attention,
+    *scratch,
+):
+    blocks, block_rows, _ = source.shape
+    columns = incoming.shape[2]
+    capacity = incoming.shape[0] // dp_count
+    chunks = block_rows // CHUNK
+    late = chunks - early_chunks
+    held = scratch[:chunks]
+    ordered = scratch[chunks : 2 * chunks]
+    (
+        early_sem,
+        own_sem,
+        tensor_send,
+        tensor_recv,
+        place_sem,
+        dp_send,
+        dp_recv,
+        att_sem,
+        att_send,
+        att_recv,
+    ) = scratch[2 * chunks :]
+    me = lax.axis_index("dp")
+    mine = lax.axis_index("tensor")
+
+    def dp_peer(step):
+        return lax.rem(me + step, dp_count)
+
+    def tensor_peer(step):
+        return lax.rem(mine + step, tensor_count)
+
+    def tile(chunk, owner):
+        return source.at[
+            :,
+            pl.ds(chunk * CHUNK, CHUNK),
+            pl.ds(pl.multiple_of(owner * columns, 128), columns),
+        ]
+
+    def early_copy(chunk):
+        return pltpu.make_async_copy(
+            early.at[:, pl.ds(chunk * CHUNK, CHUNK), :], held[chunk], early_sem.at[chunk]
+        )
+
+    def own_copy(chunk):
+        return pltpu.make_async_copy(
+            tile(chunk, mine),
+            held[chunk].at[pl.ds(mine * blocks, blocks)],
+            own_sem.at[chunk - early_chunks],
+        )
+
+    def tensor_copy(chunk, step):
+        return pltpu.make_async_remote_copy(
+            src_ref=tile(chunk, tensor_peer(step)),
+            dst_ref=held[chunk].at[pl.ds(mine * blocks, blocks)],
+            send_sem=tensor_send.at[chunk - early_chunks, step],
+            recv_sem=tensor_recv.at[chunk - early_chunks, step],
+            device_id={"tensor": tensor_peer(step)},
+            device_id_type=pl.DeviceIdType.MESH,
+        )
+
+    def place(chunk):
+        return incoming.at[pl.ds(me * capacity, capacity), pl.ds(chunk * CHUNK, CHUNK), :]
+
+    def place_copy(chunk):
+        return pltpu.make_async_copy(
+            ordered[chunk].at[pl.ds(me * capacity, capacity)], place(chunk), place_sem.at[chunk]
+        )
+
+    def dp_copy(chunk, step):
+        return pltpu.make_async_remote_copy(
+            src_ref=ordered[chunk].at[pl.ds(dp_peer(step) * capacity, capacity)],
+            dst_ref=place(chunk),
+            send_sem=dp_send.at[chunk, step],
+            recv_sem=dp_recv.at[chunk, step],
+            device_id={"dp": dp_peer(step)},
+            device_id_type=pl.DeviceIdType.MESH,
+        )
+
+    def att_copy(step):
+        return pltpu.make_async_remote_copy(
+            src_ref=summed.at[dp_peer(step)],
+            dst_ref=attention.at[me],
+            send_sem=att_send.at[step],
+            recv_sem=att_recv.at[step],
+            device_id={"dp": dp_peer(step)},
+            device_id_type=pl.DeviceIdType.MESH,
+        )
+
+    def start_tensor(chunk):
+        for step in range(1, tensor_count):
+            tensor_copy(chunk, step).start()
+        own_copy(chunk).start()
+
+    barrier = pltpu.get_barrier_semaphore()
+    for step in range(1, dp_count):
+        pl.semaphore_signal(
+            barrier, inc=1, device_id={"dp": dp_peer(step)}, device_id_type=pl.DeviceIdType.MESH
+        )
+    for step in range(1, tensor_count):
+        pl.semaphore_signal(
+            barrier,
+            inc=1,
+            device_id={"tensor": tensor_peer(step)},
+            device_id_type=pl.DeviceIdType.MESH,
+        )
+    pl.semaphore_wait(barrier, dp_count - 1 + tensor_count - 1)
+
+    for chunk in range(early_chunks, min(early_chunks + AHEAD, chunks)):
+        start_tensor(chunk)
+    for chunk in range(early_chunks):
+        early_copy(chunk).start()
+    att_own = pltpu.make_async_copy(summed.at[me], attention.at[me], att_sem)
+    att_own.start()
+    lax.fori_loop(1, dp_count, lambda step, _: (att_copy(step).start(), None)[1], None)
+
+    for chunk in range(chunks):
+        if chunk < early_chunks:
+            early_copy(chunk).wait()
+        else:
+            own_copy(chunk).wait()
+            for step in range(1, tensor_count):
+                tensor_copy(chunk, step).wait_recv()
+            if chunk + AHEAD < chunks:
+                start_tensor(chunk + AHEAD)
+
+        def reorder(slot, _, chunk=chunk):
+            ordered[chunk][slot] = held[chunk][send_index[slot]]
+
+        lax.fori_loop(0, dp_count * capacity, reorder, None)
+        lax.fori_loop(
+            1, dp_count, lambda step, _, chunk=chunk: (dp_copy(chunk, step).start(), None)[1], None
+        )
+        place_copy(chunk).start()
+
+    att_own.wait()
+    lax.fori_loop(1, dp_count, lambda step, _: (att_copy(step).wait(), None)[1], None)
+    for chunk in range(chunks):
+        if chunk >= early_chunks:
+            for step in range(1, tensor_count):
+                tensor_copy(chunk, step).wait_send()
+        place_copy(chunk).wait()
+        lax.fori_loop(
+            1, dp_count, lambda step, _, chunk=chunk: (dp_copy(chunk, step).wait(), None)[1], None
+        )
+
+
+def route(send_index, source, early, summed, dp_count, tensor_count, capacity):
+    blocks, block_rows, width = source.shape
+    group_size = blocks * tensor_count
+    columns = width // tensor_count
+    chunks = block_rows // CHUNK
+    early_chunks = early.shape[1] // CHUNK
+    late = chunks - early_chunks
+    slots = dp_count * capacity
+    anywhere = pl.BlockSpec(memory_space=pl.ANY)
+    dma = pltpu.SemaphoreType.DMA
+    return pl.pallas_call(
+        functools.partial(route_kernel, dp_count, tensor_count, early_chunks),
+        out_shape=(
+            jax.ShapeDtypeStruct((slots, block_rows, columns), jnp.bfloat16),
+            jax.ShapeDtypeStruct(summed.shape, summed.dtype),
+        ),
+        in_specs=[pl.BlockSpec(memory_space=pltpu.SMEM), anywhere, anywhere, anywhere],
+        out_specs=(anywhere, anywhere),
+        scratch_shapes=[pltpu.VMEM((group_size, CHUNK, columns), jnp.bfloat16)] * chunks
+        + [pltpu.VMEM((slots, CHUNK, columns), jnp.bfloat16)] * chunks
+        + [
+            dma((early_chunks,)),
+            dma((late,)),
+            dma((late, tensor_count)),
+            dma((late, tensor_count)),
+            dma((chunks,)),
+            dma((chunks, dp_count)),
+            dma((chunks, dp_count)),
+            dma,
+            dma((dp_count,)),
+            dma((dp_count,)),
+        ],
+        compiler_params=pltpu.CompilerParams(
+            collective_id=0, has_side_effects=True, vmem_limit_bytes=44 * 1024 * 1024
+        ),
+        cost_estimate=pl.CostEstimate(
+            flops=0, bytes_accessed=4 * slots * block_rows * columns, transcendentals=0
+        ),
+        name="route",
+    )(send_index, source, early, summed)
+
+
+def put_kernel(slot_of, block, out):
+    out[...] = block[...]
+
+
+def put(slot_of, incoming):
+    group_size = slot_of.shape[0]
+    _, block_rows, columns = incoming.shape
+    return pl.pallas_call(
+        put_kernel,
+        out_shape=jax.ShapeDtypeStruct((group_size, block_rows, columns), jnp.bfloat16),
+        grid_spec=pltpu.PrefetchScalarGridSpec(
+            num_scalar_prefetch=1,
+            grid=(group_size,),
+            in_specs=[
+                pl.BlockSpec((1, block_rows, columns), lambda place, slots: (slots[place], 0, 0))
+            ],
+            out_specs=pl.BlockSpec((1, block_rows, columns), lambda place, slots: (place, 0, 0)),
+        ),
+        compiler_params=pltpu.CompilerParams(vmem_limit_bytes=16 * 1024 * 1024),
+        name="put",
+    )(slot_of, incoming)
+
+
+def routing_tables(block_ids, dp_count):
+    group_size = block_ids.shape[0]
     capacity = max(1, group_size // dp_count)
-    mine_dp = lax.axis_index("dp")
-    target = block_ids // group_size
-    onehot = (target[:, None] == jnp.arange(dp_count, dtype=jnp.int32)[None, :]).astype(jnp.int32)
-    arrival = jnp.sum((jnp.cumsum(onehot, axis=0) - onehot) * onehot, axis=1)
-    slot_index = target * capacity + arrival
-    select = jnp.arange(dp_count * capacity, dtype=jnp.int32)[:, None] == slot_index[None, :]
-    outgoing = jnp.einsum(
-        "sb,brc->src", select.astype(jnp.bfloat16), columns, preferred_element_type=jnp.float32
-    ).astype(jnp.bfloat16)
-    outgoing_ids = jnp.sum(jnp.where(select, block_ids[None, :] + 1, 0), axis=1) - 1
-    incoming, incoming_ids = (
-        lax.all_to_all(outgoing, "dp", split_axis=0, concat_axis=0, tiled=True),
-        lax.all_to_all(outgoing_ids, "dp", split_axis=0, concat_axis=0, tiled=True),
-    )
-    position = incoming_ids - mine_dp * group_size
-    place_table = (jnp.arange(group_size, dtype=jnp.int32)[:, None] == position[None, :]).astype(
-        jnp.bfloat16
-    )
-    placed = jnp.einsum(
-        "gs,src->grc", place_table, incoming, preferred_element_type=jnp.float32
-    ).astype(jnp.bfloat16)
-    return placed.reshape(group_size * placed.shape[1], placed.shape[2])
+    me = lax.axis_index("dp")
+    numbers = lax.all_gather(block_ids, "dp", axis=0)
+    target = numbers // group_size
+    earlier = jnp.arange(group_size)[:, None] > jnp.arange(group_size)[None, :]
+    same = (target[:, :, None] == target[:, None, :]) & earlier[None]
+    arrival = jnp.sum(same.astype(jnp.int32), axis=2)
+    my_slot = (target * capacity + arrival)[me]
+    slots = jnp.arange(dp_count * capacity, dtype=jnp.int32)
+    order = jnp.arange(group_size, dtype=jnp.int32)
+    send_index = jnp.sum(
+        jnp.where(slots[:, None] == my_slot[None, :], order[None, :], 0), axis=1, dtype=jnp.int32
+    )
+    from_slot = jnp.arange(dp_count, dtype=jnp.int32)[:, None] * capacity + arrival
+    wanted = numbers.reshape(-1)[None, :] == (me * group_size + order)[:, None]
+    slot_of = jnp.sum(
+        jnp.where(wanted, from_slot.reshape(-1)[None, :], 0), axis=1, dtype=jnp.int32
+    )
+    return send_index, slot_of, capacity
 
 
 def on_device(
@@ -85,6 +308,19 @@
     block_ids,
 ):
     rows_dev = hidden.shape[0]
+    dp_count = lax.axis_size("dp")
+    tensor_count = lax.axis_size("tensor")
+    blocks, _, width = next_source.shape
+    early = lax.all_to_all(
+        next_source[:, :EARLY]
+        .reshape(blocks, EARLY, tensor_count, width // tensor_count)
+        .transpose(2, 0, 1, 3),
+        "tensor",
+        split_axis=0,
+        concat_axis=0,
+        tiled=True,
+    ).reshape(tensor_count * blocks, EARLY, width // tensor_count)
+    send_index, slot_of, capacity = routing_tables(block_ids, dp_count)
     stream = hidden.astype(jnp.float32)
     meansq = jnp.mean(stream * stream, axis=-1, keepdims=True)
     normed = (stream * lax.rsqrt(meansq + 1e-05) * norm_gain.astype(jnp.float32)).astype(
@@ -112,15 +348,24 @@
         .reshape(rows_dev, keyval_weight.shape[1], keyval_weight.shape[2])
     )
     heads_out = attend(queries, new_keyval, kv_cache, cache_lengths)
-    next_weight = relayout(next_source, block_ids)
     partial_out = jnp.dot(
         lax.all_gather(heads_out, "dp", axis=0, tiled=True),
         output_weight,
         preferred_element_type=jnp.float32,
     )
-    summed = lax.psum(partial_out.astype(jnp.bfloat16), "tensor")
-    attention = lax.all_to_all(summed, "dp", split_axis=0, concat_axis=1, tiled=True)
-    mixed = (stream + attention.astype(jnp.float32)).astype(jnp.bfloat16)
+    summed = lax.psum(partial_out.astype(jnp.bfloat16), "tensor").astype(jnp.float32)
+    incoming, attention = route(
+        send_index,
+        next_source,
+        early,
+        summed.reshape(dp_count, rows_dev, -1),
+        dp_count,
+        tensor_count,
+        capacity,
+    )
+    next_weight = put(slot_of, incoming).reshape(-1, incoming.shape[2])
+    attention = attention.transpose(1, 0, 2).reshape(rows_dev, -1)
+    mixed = (stream + attention).astype(jnp.bfloat16)
     return (mixed, next_weight)
 
 

time: 778 us -> 469 us (0.60)
  the two profiles are of different devices: /device:TPU:0 before, /device:TPU:25 now
where the time goes in v1:
time: 469 us; the launch traced here: 467 us
  Pallas kernels  268 us (57%)
  waiting for transfers between devices  108 us (23%)
  matrix products  25.4 us (5%)
  blocking collectives  17.7 us (4%)
  local copies, waits for them, and re-layouts  16.3 us (3%)
  between operations  14.9 us (3%)
  starting transfers between devices  9.86 us (2%)
  other arithmetic  7.44 us (2%)
    pallas_call x1, Pallas kernels, route(): pl.pallas_call(functools.partial(route_kernel, dp_count, tensor_count, ea...  258 us
    psum x1, waiting for transfers between devices, on_device(): lax.psum(partial_out.astype(jnp.bfloat16), 'tensor').astype(jnp.float32)  74.1 us
    reduce_scatter x1, waiting for transfers between devices, on_device(): lax.psum_scatter(jnp.concatenate([jnp.dot(pieces, query_weight, preferred...  34 us
    all_gather x1, blocking collectives, on_device(): lax.all_gather(heads_out, 'dp', axis=0, tiled=True)  10.5 us
    dot_general x1, matrix products, on_device(): jnp.dot(lax.all_gather(heads_out, 'dp', axis=0, tiled=True), output_weigh...  9.51 us
  transfers between devices with their start and end apart: 4, of which 2 were waited for; matrix products, arithmetic and copies ran while one was open for 8% of the time, Pallas kernels for 0%

profile of v1, /device:TPU:25, one launch (start us, length us, event | category | flops | bytes accessed | tf_op | source)
XLA Modules:
  0.0 467.2 jit_solution(13157869108695838620)
XLA Ops:
  7.2 1.2 fusion.18
  8.4 0.8 convert_element_type.41
  9.1 1.8 fusion.20
  10.9 4.4 all-to-all-start.1
  15.3 2.8 slice-done
  18.1 3.1 copy.32
  21.2 5.4 %all-to-all-start = ((bf16[4,4,48,4096]{3,2,1,0:T(8,128)(2,1)}), bf16[4,4,48,4096]{3,2,1,0:T(8,128)(2,1)}, u32[]{:S(2)}, u32[]{:S(2)}) async-start(bf16[4,4,48,4096]{3,2,1,0:T(8,128)(2,1)} %bitcast.44), calls=%async_computation | async-start | bytes 12582912 | tf_op jit(solution)/shard_map/all_to_all | solution.py:314
  28.2 7.2 %all-reduce = s32[128]{0:T(128)S(1)} all-reduce(s32[128]{0:T(128)S(1)} %dynamic-update-slice), channel_id=2, replica_groups=mesh['dp'=8,'tensor'=4] {'dp'}, use_global_device_ids=true, to_apply=%add | all-reduce | flops 128 | bytes 1024
  35.5 2.0 copy.20
  38.0 8.8 %convolution_convert_fusion = bf16[64,4096]{1,0:T(8,128)(2,1)S(1)} fusion(bf16[2048,4096]{1,0:T(8,128)(2,1)} %param.11, bf16[8,8,2048]{2,0,1:T(8,128)(2,1)S(1)} %all-to-all-done.1), kind=kOutput, calls=%fused_computation.1 | convolution fusion | flops 1074003968 | bytes 17563648 | tf_op jit(solution)/shard_map/dot_general | solution.py:335
  46.8 0.8 pad_maximum_fusion
  48.2 34.0 %reduce-scatter.2.cloned.1.call-done = bf16[8,4608]{1,0:T(8,128)(2,1)} async-done(((bf16[64,4608]{1,0:T(8,128)(2,1)}), bf16[8,4608]{1,0:T(8,128)(2,1)}) %reduce-scatter.2.cloned.1.call-update) | async-done | bytes 73744 | tf_op jit(solution)/shard_map/reduce_scatter | solution.py:332
  82.2 0.7 slice.31
  82.9 0.8 slice.30
  83.9 3.5 fusion.34
  87.8 3.0 fusion.14
  90.8 10.5 %all_gather.11 = bf16[64,4096]{1,0:T(8,128)(2,1)S(1)} all-gather(bf16[8,4096]{1,0:T(8,128)(2,1)S(1)} %bitcast.48), channel_id=1, replica_groups=mesh['dp'=8,'tensor'=4] {'dp'}, dimensions={0}, use_global_device_ids=true | all-gather | bytes 589824 | tf_op jit(solution)/shard_map/all_gather | solution.py:352
  101.3 9.5 %fusion.4 = bf16[8,8,2048]{2,1,0:T(8,128)(2,1)} fusion(bf16[64,4096]{1,0:T(8,128)(2,1)S(1)} %all_gather.11, bf16[4096,2048]{1,0:T(8,128)(2,1)} %param.13), kind=kOutput, calls=%fused_computation.7 | convolution fusion | flops 1073872896 | bytes 17563648 | tf_op jit(solution)/shard_map/dot_general | solution.py:351
  111.2 74.1 %all-reduce.3.cloned.1.call-done = bf16[8,8,2048]{2,1,0:T(8,128)(2,1)} async-done(((bf16[8,8,2048]{2,1,0:T(8,128)(2,1)}), bf16[8,8,2048]{2,1,0:T(8,128)(2,1)}) %all-reduce.3.cloned.1.call-update) | async-done | bytes 262160 | tf_op jit(solution)/shard_map/psum | solution.py:356
  185.3 1.0 reshape.110.summed
  186.3 258.3 %route.1 = (bf16[16,128,4096]{2,1,0:T(8,128)(2,1)}, f32[8,8,2048]{2,1,0:T(8,128)S(1)}) custom-call(s32[16]{0:T(128)S(1)} %select_reduce_fusion.1.send_index, bf16[4,128,16384]{2,1,0:T(8,128)(2,1)} %source.1, bf16[16,48,4096]{2,1,0:T(8,128)(2,1)} %bitcast.3.early, f32[8,8,2048]{2,1,0:T(8,128)S(1)} %reshape.110.summed), custom_call_target="tpu_custom_call" | custom-call | bytes 33554432 | tf_op jit(solution)/shard_map/route/pallas_call | solution.py:221
  444.7 0.7 fusion.21
  445.4 5.8 %copy-done = bf16[16,128,4096]{2,1,0:T(8,128)(2,1)S(1)} copy-done((bf16[16,128,4096]{2,1,0:T(8,128)(2,1)S(1)}, bf16[16,128,4096]{2,1,0:T(8,128)(2,1)}, u32[]{:S(2)}) %copy-start) | copy-done | bytes 16777240
  451.2 9.2 %put.1 = bf16[16,128,4096]{2,1,0:T(8,128)(2,1)} custom-call(s32[16]{0:T(128)S(1)} %select_reduce_fusion.slot_of, bf16[16,128,4096]{2,1,0:T(8,128)(2,1)S(1)} %copy-done), custom_call_target="tpu_custom_call" | custom-call | tf_op jit(solution)/shard_map/put/pallas_call | solution.py:260
  (40 shorter events, 2.9 us)
Async XLA Ops:
  10.9 10.3 %all-to-all-start.1 = ((bf16[8,8,2048]{2,0,1:T(8,128)(2,1)}), bf16[8,8,2048]{2,0,1:T(8,128)(2,1)S(1)}, u32[]{:S(2)}, u32[]{:S(2)}) async-start(bf16[8,8,2048]{2,0,1:T(8,128)(2,1)} %bitcast.4), calls=%async_computation.1 | async-start | bytes 524288 | tf_op jit(solution)/shard_map/all_to_all | solution.py:329
  15.3 2.8 slice-start
  21.2 5.5 %copy-start.4 = (u32[32]{0:T(128)S(1)}, u32[32]{0:T(128)}, u32[]{:S(2)}) copy-start(u32[32]{0:T(128)} %constant.46) | copy-start | bytes 388
  21.2 6.7 %copy-start.3 = (s32[16]{0:T(128)S(1)}, s32[16]{0:T(128)}, u32[]{:S(2)}) copy-start(s32[16]{0:T(128)} %param.17) | copy-start | bytes 196
  21.2 165.1 %all-to-all-start = ((bf16[4,4,48,4096]{3,2,1,0:T(8,128)(2,1)}), bf16[4,4,48,4096]{3,2,1,0:T(8,128)(2,1)}, u32[]{:S(2)}, u32[]{:S(2)}) async-start(bf16[4,4,48,4096]{3,2,1,0:T(8,128)(2,1)} %bitcast.44), calls=%async_computation | async-start | bytes 12582912 | tf_op jit(solution)/shard_map/all_to_all | solution.py:314
  26.6 55.6 %reduce-scatter.2.cloned.1.call-start = ((), (), s32[]{:S(2)}) async-start(), calls=%async_computation.3 | async-start | bytes 663552 | tf_op jit(solution)/shard_map/reduce_scatter | solution.py:332
  38.0 10.0 %copy-start.2 = (s32[8]{0:T(128)S(1)}, s32[8]{0:T(128)}, u32[]{:S(2)}) copy-start(s32[8]{0:T(128)} %param.15) | copy-start | bytes 100
  47.7 137.6 %all-reduce.3.cloned.1.call-start = ((), (), s32[]{:S(2)}) async-start(), calls=%async_computation.4 | async-start | bytes 524288 | tf_op jit(solution)/shard_map/psum | solution.py:356
  186.3 258.4 %copy-start.1 = (bf16[8,16384]{1,0:T(8,128)(2,1)S(1)}, bf16[8,16384]{1,0:T(8,128)(2,1)}, u32[]{:S(2)}) copy-start(bf16[8,16384]{1,0:T(8,128)(2,1)} %param.9) | copy-start | bytes 786436
  445.4 5.8 %copy-start = (bf16[16,128,4096]{2,1,0:T(8,128)(2,1)S(1)}, bf16[16,128,4096]{2,1,0:T(8,128)(2,1)}, u32[]{:S(2)}) copy-start(bf16[16,128,4096]{2,1,0:T(8,128)(2,1)} %get-tuple-element.5.block) | copy-start | bytes 50331652
Sparse Core Ops, SparseCore 0:
  47.8 34.3 reduce-scatter.1
  110.9 74.3 all-reduce.2

commit v2 on v1

--- a/solution.py
+++ b/solution.py
@@ -49,18 +49,25 @@
 
 
 CHUNK = 16
-EARLY = 48
+EARLY = 32
 AHEAD = 3
+TAIL_PARTS = 4
+
+
+def chunk_list(block_rows, early_rows, columns):
+    parts = [(row, 0, columns) for row in range(0, block_rows - CHUNK, CHUNK)]
+    width = columns // TAIL_PARTS
+    parts += [(block_rows - CHUNK, width * part, width) for part in range(TAIL_PARTS)]
+    return parts, early_rows // CHUNK
 
 
 def route_kernel(
     dp_count,
     tensor_count,
-    early_chunks,
     send_index,
     source,
     early,
-    summed,
+    partial,
     incoming,
     attention,
     *scratch,
@@ -68,11 +75,15 @@
     blocks, block_rows, _ = source.shape
     columns = incoming.shape[2]
     capacity = incoming.shape[0] // dp_count
-    chunks = block_rows // CHUNK
-    late = chunks - early_chunks
+    parts, early_chunks = chunk_list(block_rows, early.shape[1], columns)
+    chunks = len(parts)
     held = scratch[:chunks]
     ordered = scratch[chunks : 2 * chunks]
     (
+        gathered,
+        outgoing,
+        arrived,
+        total,
         early_sem,
         own_sem,
         tensor_send,
@@ -83,7 +94,13 @@
         att_sem,
         att_send,
         att_recv,
+        reduce_send,
+        reduce_recv,
+        share_sem,
+        share_send,
+        share_recv,
     ) = scratch[2 * chunks :]
+    share = dp_count // tensor_count
     me = lax.axis_index("dp")
     mine = lax.axis_index("tensor")
 
@@ -94,15 +111,16 @@
         return lax.rem(mine + step, tensor_count)
 
     def tile(chunk, owner):
+        row, column, width = parts[chunk]
         return source.at[
             :,
-            pl.ds(chunk * CHUNK, CHUNK),
-            pl.ds(pl.multiple_of(owner * columns, 128), columns),
+            pl.ds(row, CHUNK),
+            pl.ds(pl.multiple_of(owner * columns + column, 128), width),
         ]
 
     def early_copy(chunk):
         return pltpu.make_async_copy(
-            early.at[:, pl.ds(chunk * CHUNK, CHUNK), :], held[chunk], early_sem.at[chunk]
+            early.at[:, pl.ds(parts[chunk][0], CHUNK), :], held[chunk], early_sem.at[chunk]
         )
 
     def own_copy(chunk):
@@ -123,7 +141,10 @@
         )
 
     def place(chunk):
-        return incoming.at[pl.ds(me * capacity, capacity), pl.ds(chunk * CHUNK, CHUNK), :]
+        row, column, width = parts[chunk]
+        return incoming.at[
+            pl.ds(me * capacity, capacity), pl.ds(row, CHUNK), pl.ds(column, width)
+        ]
 
     def place_copy(chunk):
         return pltpu.make_async_copy(
@@ -142,13 +163,53 @@
 
     def att_copy(step):
         return pltpu.make_async_remote_copy(
-            src_ref=summed.at[dp_peer(step)],
-            dst_ref=attention.at[me],
+            src_ref=partial.at[dp_peer(step)],
+            dst_ref=gathered.at[me],
             send_sem=att_send.at[step],
             recv_sem=att_recv.at[step],
             device_id={"dp": dp_peer(step)},
             device_id_type=pl.DeviceIdType.MESH,
         )
+
+    def reduce_copy(step):
+        return pltpu.make_async_remote_copy(
+            src_ref=outgoing.at[tensor_peer(step)],
+            dst_ref=arrived.at[mine],
+            send_sem=reduce_send.at[step],
+            recv_sem=reduce_recv.at[step],
+            device_id={"tensor": tensor_peer(step)},
+            device_id_type=pl.DeviceIdType.MESH,
+        )
+
+    def share_copy(step):
+        return pltpu.make_async_remote_copy(
+            src_ref=total,
+            dst_ref=attention.at[mine],
+            send_sem=share_send.at[step],
+            recv_sem=share_recv.at[step],
+            device_id={"tensor": tensor_peer(step)},
+            device_id_type=pl.DeviceIdType.MESH,
+        )
+
+    def start_reduce():
+        att_own.wait()
+        lax.fori_loop(1, dp_count, lambda step, _: (att_copy(step).wait(), None)[1], None)
+        for owner in range(tensor_count):
+            rows = gathered[owner * share : (owner + 1) * share]
+            outgoing[owner] = rows.reshape(outgoing.shape[1:]).astype(outgoing.dtype)
+        for step in range(1, tensor_count):
+            reduce_copy(step).start()
+
+    def start_share():
+        for step in range(1, tensor_count):
+            reduce_copy(step).wait()
+        value = outgoing[mine].astype(jnp.float32)
+        for step in range(1, tensor_count):
+            value += arrived[tensor_peer(step)].astype(jnp.float32)
+        total[...] = value.astype(total.dtype)
+        for step in range(1, tensor_count):
+            share_copy(step).start()
+        share_own.start()
 
     def start_tensor(chunk):
         for step in range(1, tensor_count):
@@ -173,11 +234,16 @@
         start_tensor(chunk)
     for chunk in range(early_chunks):
         early_copy(chunk).start()
-    att_own = pltpu.make_async_copy(summed.at[me], attention.at[me], att_sem)
+    att_own = pltpu.make_async_copy(partial.at[me], gathered.at[me], att_sem)
+    share_own = pltpu.make_async_copy(total, attention.at[mine], share_sem)
     att_own.start()
     lax.fori_loop(1, dp_count, lambda step, _: (att_copy(step).start(), None)[1], None)
 
     for chunk in range(chunks):
+        if chunk == early_chunks:
+            start_reduce()
+        if chunk == early_chunks + AHEAD:
+            start_share()
         if chunk < early_chunks:
             early_copy(chunk).wait()
         else:
@@ -196,8 +262,9 @@
         )
         place_copy(chunk).start()
 
-    att_own.wait()
-    lax.fori_loop(1, dp_count, lambda step, _: (att_copy(step).wait(), None)[1], None)
+    share_own.wait()
+    for step in range(1, tensor_count):
+        share_copy(step).wait()
     for chunk in range(chunks):
         if chunk >= early_chunks:
             for step in range(1, tensor_count):
@@ -208,27 +275,35 @@
         )
 
 
-def route(send_index, source, early, summed, dp_count, tensor_count, capacity):
+def route(send_index, source, early, partial, dp_count, tensor_count, capacity):
     blocks, block_rows, width = source.shape
     group_size = blocks * tensor_count
     columns = width // tensor_count
-    chunks = block_rows // CHUNK
-    early_chunks = early.shape[1] // CHUNK
+    parts, early_chunks = chunk_list(block_rows, early.shape[1], columns)
+    chunks = len(parts)
     late = chunks - early_chunks
     slots = dp_count * capacity
+    shared = (dp_count // tensor_count * partial.shape[1], partial.shape[2])
+    exchanged = (tensor_count, *shared)
     anywhere = pl.BlockSpec(memory_space=pl.ANY)
     dma = pltpu.SemaphoreType.DMA
     return pl.pallas_call(
-        functools.partial(route_kernel, dp_count, tensor_count, early_chunks),
+        functools.partial(route_kernel, dp_count, tensor_count),
         out_shape=(
             jax.ShapeDtypeStruct((slots, block_rows, columns), jnp.bfloat16),
-            jax.ShapeDtypeStruct(summed.shape, summed.dtype),
+            jax.ShapeDtypeStruct(exchanged, jnp.bfloat16),
         ),
         in_specs=[pl.BlockSpec(memory_space=pltpu.SMEM), anywhere, anywhere, anywhere],
         out_specs=(anywhere, anywhere),
-        scratch_shapes=[pltpu.VMEM((group_size, CHUNK, columns), jnp.bfloat16)] * chunks
-        + [pltpu.VMEM((slots, CHUNK, columns), jnp.bfloat16)] * chunks
+        scratch_shapes=[
+            pltpu.VMEM((group_size, CHUNK, part[2]), jnp.bfloat16) for part in parts
+        ]
+        + [pltpu.VMEM((slots, CHUNK, part[2]), jnp.bfloat16) for part in parts]
         + [
+            pltpu.VMEM(partial.shape, jnp.float32),
+            pltpu.VMEM(exchanged, jnp.bfloat16),
+            pltpu.VMEM(exchanged, jnp.bfloat16),
+            pltpu.VMEM(shared, jnp.bfloat16),
             dma((early_chunks,)),
             dma((late,)),
             dma((late, tensor_count)),
@@ -239,6 +314,11 @@
             dma,
             dma((dp_count,)),
             dma((dp_count,)),
+            dma((tensor_count,)),
+            dma((tensor_count,)),
+            dma,
+            dma((tensor_count,)),
+            dma((tensor_count,)),
         ],
         compiler_params=pltpu.CompilerParams(
             collective_id=0, has_side_effects=True, vmem_limit_bytes=44 * 1024 * 1024
@@ -247,7 +327,7 @@
             flops=0, bytes_accessed=4 * slots * block_rows * columns, transcendentals=0
         ),
         name="route",
-    )(send_index, source, early, summed)
+    )(send_index, source, early, partial)
 
 
 def put_kernel(slot_of, block, out):
@@ -268,7 +348,7 @@
             ],
             out_specs=pl.BlockSpec((1, block_rows, columns), lambda place, slots: (place, 0, 0)),
         ),
-        compiler_params=pltpu.CompilerParams(vmem_limit_bytes=16 * 1024 * 1024),
+        compiler_params=pltpu.CompilerParams(vmem_limit_bytes=52 * 1024 * 1024),
         name="put",
     )(slot_of, incoming)
 
@@ -353,18 +433,18 @@
         output_weight,
         preferred_element_type=jnp.float32,
     )
-    summed = lax.psum(partial_out.astype(jnp.bfloat16), "tensor").astype(jnp.float32)
     incoming, attention = route(
         send_index,
         next_source,
         early,
-        summed.reshape(dp_count, rows_dev, -1),
+        partial_out.reshape(dp_count, rows_dev, -1),
         dp_count,
         tensor_count,
         capacity,
     )
     next_weight = put(slot_of, incoming).reshape(-1, incoming.shape[2])
-    attention = attention.transpose(1, 0, 2).reshape(rows_dev, -1)
+    attention = attention.reshape(dp_count, rows_dev, -1).transpose(1, 0, 2)
+    attention = attention.reshape(rows_dev, -1).astype(jnp.float32)
     mixed = (stream + attention).astype(jnp.bfloat16)
     return (mixed, next_weight)
 

time: 469 us -> 446 us (0.951)
  waiting for transfers between devices: 108 us -> 43.4 us
  Pallas kernels: 268 us -> 322 us
  local copies, waits for them, and re-layouts: 16.3 us -> 7.53 us
    psum x1 -> x0, waiting for transfers between devices: 74.1 us -> none  [on_device(): lax.psum(partial_out.astype(jnp.bfloat16), 'tensor').astype(jnp.float32)]
    pallas_call x1, Pallas kernels: 258 us -> 304 us  [route(): pl.pallas_call(functools.partial(route_kernel, dp_count, tensor_count), o...]
    pallas_call x1, Pallas kernels: 9.2 us -> 18 us  [put(): pl.pallas_call(put_kernel, out_shape=jax.ShapeDtypeStruct((group_size, bl...]
    unnamed x15, local copies, waits for them, and re-layouts: 8.69 us -> 1.34 us
    all_to_all x1, waiting for transfers between devices: 0.01 us -> 7.06 us  [on_device(): lax.all_to_all(next_source[:, :EARLY].reshape(blocks, EARLY, tensor_count...]
  transfers between devices with their start and end apart: 4 -> 3, of which waited for: 2 -> 3; matrix products, arithmetic and copies ran while one was open for 8% -> 7% of each run, Pallas kernels for 0% -> 0%
where the time goes in v2:
time: 446 us; the launch traced here: 445 us
  Pallas kernels  322 us (72%)
  waiting for transfers between devices  43.4 us (10%)
  matrix products  24.7 us (6%)
  blocking collectives  17 us (4%)
  between operations  14.9 us (3%)
  starting transfers between devices  9.28 us (2%)
  local copies, waits for them, and re-layouts  7.53 us (2%)
  other arithmetic  6.5 us (1%)
    pallas_call x1, Pallas kernels, route(): pl.pallas_call(functools.partial(route_kernel, dp_count, tensor_count), o...  304 us
    reduce_scatter x1, waiting for transfers between devices, on_device(): lax.psum_scatter(jnp.concatenate([jnp.dot(pieces, query_weight, preferred...  35.1 us
    pallas_call x1, Pallas kernels, put(): pl.pallas_call(put_kernel, out_shape=jax.ShapeDtypeStruct((group_size, bl...  18 us
    all_gather x1, blocking collectives, on_device(): lax.all_gather(heads_out, 'dp', axis=0, tiled=True)  10.8 us
  transfers between devices with their start and end apart: 3, of which 3 were waited for; matrix products, arithmetic and copies ran while one was open for 7% of the time, Pallas kernels for 0%

profile of v2, /device:TPU:25, one launch (start us, length us, event | category | flops | bytes accessed | tf_op | source)
XLA Modules:
  0.0 444.9 jit_solution(11206075781382091829)
XLA Ops:
  7.2 1.2 fusion.17
  8.4 0.8 convert_element_type.49
  9.1 1.8 fusion.19
  10.9 4.4 all-to-all-start.1
  15.3 2.2 slice-done
  17.5 2.3 copy.32
  19.8 1.1 all-to-all-done.1
  20.9 4.8 %all-to-all-start = ((bf16[4,4,32,4096]{3,2,1,0:T(8,128)(2,1)}), bf16[4,4,32,4096]{3,2,1,0:T(8,128)(2,1)}, u32[]{:S(2)}, u32[]{:S(2)}) async-start(bf16[4,4,32,4096]{3,2,1,0:T(8,128)(2,1)} %bitcast.47), calls=%async_computation | async-start | bytes 8388608 | tf_op jit(solution)/shard_map/all_to_all | solution.py:394
  25.8 0.6 dynamic-slice
  27.3 6.2 %all-reduce = s32[128]{0:T(128)S(1)} all-reduce(s32[128]{0:T(128)S(1)} %dynamic-update-slice), channel_id=2, replica_groups=mesh['dp'=8,'tensor'=4] {'dp'}, use_global_device_ids=true, to_apply=%add | all-reduce | flops 128 | bytes 1024
  34.4 0.5 convolution_convert_fusion.1
  34.9 8.8 %convolution_convert_fusion = bf16[64,4096]{1,0:T(8,128)(2,1)S(1)} fusion(bf16[2048,4096]{1,0:T(8,128)(2,1)} %param.11, bf16[8,8,2048]{2,0,1:T(8,128)(2,1)S(1)} %all-to-all-done.1), kind=kOutput, calls=%fused_computation | convolution fusion | flops 1074003968 | bytes 17563648 | tf_op jit(solution)/shard_map/dot_general | solution.py:415
  43.7 0.8 pad_maximum_fusion
  45.2 35.1 %reduce-scatter.2.cloned.1.call-done = bf16[8,4608]{1,0:T(8,128)(2,1)} async-done(((bf16[64,4608]{1,0:T(8,128)(2,1)}), bf16[8,4608]{1,0:T(8,128)(2,1)}) %reduce-scatter.2.cloned.1.call-update) | async-done | bytes 73744 | tf_op jit(solution)/shard_map/reduce_scatter | solution.py:412
  80.3 0.7 slice.31
  81.0 0.8 slice.30
  82.0 3.5 fusion.33
  85.9 3.0 fusion.13
  88.9 10.8 %all_gather.11 = bf16[64,4096]{1,0:T(8,128)(2,1)S(1)} all-gather(bf16[8,4096]{1,0:T(8,128)(2,1)S(1)} %bitcast.51), channel_id=1, replica_groups=mesh['dp'=8,'tensor'=4] {'dp'}, dimensions={0}, use_global_device_ids=true | all-gather | bytes 589824 | tf_op jit(solution)/shard_map/all_gather | solution.py:432
  99.6 8.8 %convolution_bitcast_fusion.partial = f32[8,8,2048]{2,1,0:T(8,128)S(1)} fusion(bf16[64,4096]{1,0:T(8,128)(2,1)S(1)} %all_gather.11, bf16[4096,2048]{1,0:T(8,128)(2,1)} %param.13), kind=kOutput, calls=%fused_computation.6 | convolution fusion | flops 1073741824 | bytes 17825792 | tf_op jit(solution)/shard_map/dot_general | solution.py:431
  108.5 7.1 %all-to-all-done = bf16[4,4,32,4096]{3,2,1,0:T(8,128)(2,1)} async-done(((bf16[4,4,32,4096]{3,2,1,0:T(8,128)(2,1)}), bf16[4,4,32,4096]{3,2,1,0:T(8,128)(2,1)}, u32[]{:S(2)}, u32[]{:S(2)}) %all-to-all-start) | async-done | bytes 4194336 | tf_op jit(solution)/shard_map/all_to_all | solution.py:394
  115.5 303.7 %route.1 = (bf16[16,128,4096]{2,1,0:T(8,128)(2,1)}, bf16[4,16,2048]{2,1,0:T(8,128)(2,1)S(1)}) custom-call(s32[16]{0:T(128)S(1)} %select_reduce_fusion.1.send_index, bf16[4,128,16384]{2,1,0:T(8,128)(2,1)} %source.1, bf16[16,32,4096]{2,1,0:T(8,128)(2,1)} %bitcast.3.early, f32[8,8,2048]{2,1,0:T(8,128)S(1)} %convolution_bitcast_fusion.partial), custom_call_target="tpu_custom_call" | custom-call | bytes 33554432 | tf_op jit(solution)/shard_map/route/pallas_call | solution.py:290
  419.3 0.7 fusion.20
  420.1 18.0 %put.1 = bf16[16,128,4096]{2,1,0:T(8,128)(2,1)} custom-call(s32[16]{0:T(128)S(1)} %select_reduce_fusion.slot_of, bf16[16,128,4096]{2,1,0:T(8,128)(2,1)} %get-tuple-element.5.block), custom_call_target="tpu_custom_call" | custom-call | tf_op jit(solution)/shard_map/put/pallas_call | solution.py:340
  (37 shorter events, 2.3 us)
Async XLA Ops:
  10.9 10.0 %all-to-all-start.1 = ((bf16[8,8,2048]{2,0,1:T(8,128)(2,1)}), bf16[8,8,2048]{2,0,1:T(8,128)(2,1)S(1)}, u32[]{:S(2)}, u32[]{:S(2)}) async-start(bf16[8,8,2048]{2,0,1:T(8,128)(2,1)} %bitcast.4), calls=%async_computation.1 | async-start | bytes 524288 | tf_op jit(solution)/shard_map/all_to_all | solution.py:409
  15.3 2.2 slice-start
  17.5 8.3 %copy-start.4 = (u32[32]{0:T(128)S(1)}, u32[32]{0:T(128)}, u32[]{:S(2)}) copy-start(u32[32]{0:T(128)} %constant.46) | copy-start | bytes 388
  17.5 9.6 %copy-start.3 = (s32[16]{0:T(128)S(1)}, s32[16]{0:T(128)}, u32[]{:S(2)}) copy-start(s32[16]{0:T(128)} %param.17) | copy-start | bytes 196
  17.5 16.1 %copy-start.1 = (bf16[2048,2,256]{2,1,0:T(2,128)(2,1)S(1)}, bf16[2048,2,256]{2,1,0:T(2,128)(2,1)}, u32[]{:S(2)}) copy-start(bf16[2048,2,256]{2,1,0:T(2,128)(2,1)} %param.12) | copy-start | bytes 6291460
  20.9 94.6 %all-to-all-start = ((bf16[4,4,32,4096]{3,2,1,0:T(8,128)(2,1)}), bf16[4,4,32,4096]{3,2,1,0:T(8,128)(2,1)}, u32[]{:S(2)}, u32[]{:S(2)}) async-start(bf16[4,4,32,4096]{3,2,1,0:T(8,128)(2,1)} %bitcast.47), calls=%async_computation | async-start | bytes 8388608 | tf_op jit(solution)/shard_map/all_to_all | solution.py:394
  25.8 54.5 %reduce-scatter.2.cloned.1.call-start = ((), (), s32[]{:S(2)}) async-start(), calls=%async_computation.3 | async-start | bytes 663552 | tf_op jit(solution)/shard_map/reduce_scatter | solution.py:412
  34.9 10.2 %copy-start.2 = (s32[8]{0:T(128)S(1)}, s32[8]{0:T(128)}, u32[]{:S(2)}) copy-start(s32[8]{0:T(128)} %param.15) | copy-start | bytes 100
  115.5 303.8 %copy-start = (bf16[8,16384]{1,0:T(8,128)(2,1)S(1)}, bf16[8,16384]{1,0:T(8,128)(2,1)}, u32[]{:S(2)}) copy-start(bf16[8,16384]{1,0:T(8,128)(2,1)} %param.9) | copy-start | bytes 786436
Sparse Core Ops, SparseCore 0:
  44.7 35.5 reduce-scatter.1

commit v3 on v2

--- a/solution.py
+++ b/solution.py
@@ -330,25 +330,43 @@
     )(send_index, source, early, partial)
 
 
-def put_kernel(slot_of, block, out):
-    out[...] = block[...]
+def put_kernel(slot_of, incoming, out, held, read_sem, write_sem):
+    places = held.shape[0]
+
+    def read(place):
+        return pltpu.make_async_copy(
+            incoming.at[slot_of[place]], held.at[place], read_sem.at[place]
+        )
+
+    def write(place):
+        return pltpu.make_async_copy(held.at[place], out.at[place], write_sem.at[place])
+
+    for place in range(places):
+        read(place).start()
+    for place in range(places):
+        read(place).wait()
+        write(place).start()
+    for place in range(places):
+        write(place).wait()
 
 
 def put(slot_of, incoming):
     group_size = slot_of.shape[0]
-    _, block_rows, columns = incoming.shape
+    shape = (group_size, *incoming.shape[1:])
     return pl.pallas_call(
         put_kernel,
-        out_shape=jax.ShapeDtypeStruct((group_size, block_rows, columns), jnp.bfloat16),
-        grid_spec=pltpu.PrefetchScalarGridSpec(
-            num_scalar_prefetch=1,
-            grid=(group_size,),
-            in_specs=[
-                pl.BlockSpec((1, block_rows, columns), lambda place, slots: (slots[place], 0, 0))
-            ],
-            out_specs=pl.BlockSpec((1, block_rows, columns), lambda place, slots: (place, 0, 0)),
-        ),
-        compiler_params=pltpu.CompilerParams(vmem_limit_bytes=52 * 1024 * 1024),
+        out_shape=jax.ShapeDtypeStruct(shape, jnp.bfloat16),
+        in_specs=[
+            pl.BlockSpec(memory_space=pltpu.SMEM),
+            pl.BlockSpec(memory_space=pl.ANY),
+        ],
+        out_specs=pl.BlockSpec(memory_space=pl.ANY),
+        scratch_shapes=[
+            pltpu.VMEM(shape, jnp.bfloat16),
+            pltpu.SemaphoreType.DMA((group_size,)),
+            pltpu.SemaphoreType.DMA((group_size,)),
+        ],
+        compiler_params=pltpu.CompilerParams(vmem_limit_bytes=56 * 1024 * 1024),
         name="put",
     )(slot_of, incoming)
 

time: 446 us -> 440 us (0.987)
  Pallas kernels: 322 us -> 316 us
    pallas_call x1, Pallas kernels: 18 us -> 12.6 us  [put(): pl.pallas_call(put_kernel, out_shape=jax.ShapeDtypeStruct(shape, jnp.bflo...]
where the time goes in v3:
time: 440 us
  Pallas kernels  316 us (72%)
  waiting for transfers between devices  42.8 us (10%)
  matrix products  24.7 us (6%)
  blocking collectives  17 us (4%)
  between operations  14.9 us (3%)
  starting transfers between devices  9.28 us (2%)
  local copies, waits for them, and re-layouts  7.53 us (2%)
  other arithmetic  7.05 us (2%)
    pallas_call x1, Pallas kernels, route(): pl.pallas_call(functools.partial(route_kernel, dp_count, tensor_count), o...  304 us
    reduce_scatter x1, waiting for transfers between devices, on_device(): lax.psum_scatter(jnp.concatenate([jnp.dot(pieces, query_weight, preferred...  34.6 us
    pallas_call x1, Pallas kernels, put(): pl.pallas_call(put_kernel, out_shape=jax.ShapeDtypeStruct(shape, jnp.bflo...  12.6 us
    all_gather x1, blocking collectives, on_device(): lax.all_gather(heads_out, 'dp', axis=0, tiled=True)  10.8 us
    dot_general x1, matrix products, on_device(): jnp.dot(lax.all_gather(heads_out, 'dp', axis=0, tiled=True), output_weigh...  8.8 us
  transfers between devices with their start and end apart: 3, of which 3 were waited for; matrix products, arithmetic and copies ran while one was open for 7% of the time, Pallas kernels for 0%

profile of v3, /device:TPU:25, one launch (start us, length us, event | category | flops | bytes accessed | tf_op | source)
XLA Modules:
  0.0 439.6 jit_solution(8861991883472256346)
XLA Ops:
  7.2 1.2 fusion.17
  8.4 0.8 convert_element_type.49
  9.1 1.8 fusion.19
  10.9 4.4 all-to-all-start.1
  15.3 2.2 slice-done
  17.5 2.3 copy.32
  19.8 1.1 all-to-all-done.1
  20.9 4.8 %all-to-all-start = ((bf16[4,4,32,4096]{3,2,1,0:T(8,128)(2,1)}), bf16[4,4,32,4096]{3,2,1,0:T(8,128)(2,1)}, u32[]{:S(2)}, u32[]{:S(2)}) async-start(bf16[4,4,32,4096]{3,2,1,0:T(8,128)(2,1)} %bitcast.47), calls=%async_computation | async-start | bytes 8388608 | tf_op jit(solution)/shard_map/all_to_all | solution.py:412
  25.8 0.6 dynamic-slice
  27.3 6.2 %all-reduce = s32[128]{0:T(128)S(1)} all-reduce(s32[128]{0:T(128)S(1)} %dynamic-update-slice), channel_id=2, replica_groups=mesh['dp'=8,'tensor'=4] {'dp'}, use_global_device_ids=true, to_apply=%add | all-reduce | flops 128 | bytes 1024
  34.9 8.8 %convolution_convert_fusion = bf16[64,4096]{1,0:T(8,128)(2,1)S(1)} fusion(bf16[2048,4096]{1,0:T(8,128)(2,1)} %param.11, bf16[8,8,2048]{2,0,1:T(8,128)(2,1)S(1)} %all-to-all-done.1), kind=kOutput, calls=%fused_computation | convolution fusion | flops 1074003968 | bytes 17563648 | tf_op jit(solution)/shard_map/dot_general | solution.py:433
  43.7 0.8 pad_maximum_fusion
  44.9 0.7 select_reduce_fusion.slot_of
  45.7 34.6 %reduce-scatter.2.cloned.1.call-done = bf16[8,4608]{1,0:T(8,128)(2,1)} async-done(((bf16[64,4608]{1,0:T(8,128)(2,1)}), bf16[8,4608]{1,0:T(8,128)(2,1)}) %reduce-scatter.2.cloned.1.call-update) | async-done | bytes 73744 | tf_op jit(solution)/shard_map/reduce_scatter | solution.py:430
  80.3 0.7 slice.31
  81.0 0.8 slice.30
  82.0 3.5 fusion.33
  85.9 3.0 fusion.13
  88.9 10.8 %all_gather.11 = bf16[64,4096]{1,0:T(8,128)(2,1)S(1)} all-gather(bf16[8,4096]{1,0:T(8,128)(2,1)S(1)} %bitcast.51), channel_id=1, replica_groups=mesh['dp'=8,'tensor'=4] {'dp'}, dimensions={0}, use_global_device_ids=true | all-gather | bytes 589824 | tf_op jit(solution)/shard_map/all_gather | solution.py:450
  99.6 8.8 %convolution_bitcast_fusion.partial = f32[8,8,2048]{2,1,0:T(8,128)S(1)} fusion(bf16[64,4096]{1,0:T(8,128)(2,1)S(1)} %all_gather.11, bf16[4096,2048]{1,0:T(8,128)(2,1)} %param.13), kind=kOutput, calls=%fused_computation.6 | convolution fusion | flops 1073741824 | bytes 17825792 | tf_op jit(solution)/shard_map/dot_general | solution.py:449
  108.5 7.1 %all-to-all-done = bf16[4,4,32,4096]{3,2,1,0:T(8,128)(2,1)} async-done(((bf16[4,4,32,4096]{3,2,1,0:T(8,128)(2,1)}), bf16[4,4,32,4096]{3,2,1,0:T(8,128)(2,1)}, u32[]{:S(2)}, u32[]{:S(2)}) %all-to-all-start) | async-done | bytes 4194336 | tf_op jit(solution)/shard_map/all_to_all | solution.py:412
  115.5 303.7 %route.1 = (bf16[16,128,4096]{2,1,0:T(8,128)(2,1)}, bf16[4,16,2048]{2,1,0:T(8,128)(2,1)S(1)}) custom-call(s32[16]{0:T(128)S(1)} %select_reduce_fusion.1.send_index, bf16[4,128,16384]{2,1,0:T(8,128)(2,1)} %source.1, bf16[16,32,4096]{2,1,0:T(8,128)(2,1)} %bitcast.3.early, f32[8,8,2048]{2,1,0:T(8,128)S(1)} %convolution_bitcast_fusion.partial), custom_call_target="tpu_custom_call" | custom-call | bytes 33554432 | tf_op jit(solution)/shard_map/route/pallas_call | solution.py:290
  419.3 0.7 fusion.20
  420.1 12.6 %put.1 = bf16[16,128,4096]{2,1,0:T(8,128)(2,1)} custom-call(s32[16]{0:T(128)} %select_reduce_fusion.slot_of, bf16[16,128,4096]{2,1,0:T(8,128)(2,1)} %get-tuple-element.5.incoming), custom_call_target="tpu_custom_call" | custom-call | tf_op jit(solution)/shard_map/put/pallas_call | solution.py:356
  (37 shorter events, 2.6 us)
Async XLA Ops:
  10.9 10.0 %all-to-all-start.1 = ((bf16[8,8,2048]{2,0,1:T(8,128)(2,1)}), bf16[8,8,2048]{2,0,1:T(8,128)(2,1)S(1)}, u32[]{:S(2)}, u32[]{:S(2)}) async-start(bf16[8,8,2048]{2,0,1:T(8,128)(2,1)} %bitcast.4), calls=%async_computation.1 | async-start | bytes 524288 | tf_op jit(solution)/shard_map/all_to_all | solution.py:427
  15.3 2.2 slice-start
  17.5 8.3 %copy-start.4 = (u32[32]{0:T(128)S(1)}, u32[32]{0:T(128)}, u32[]{:S(2)}) copy-start(u32[32]{0:T(128)} %constant.46) | copy-start | bytes 388
  17.5 9.6 %copy-start.3 = (s32[16]{0:T(128)S(1)}, s32[16]{0:T(128)}, u32[]{:S(2)}) copy-start(s32[16]{0:T(128)} %param.17) | copy-start | bytes 196
  17.5 16.1 %copy-start.1 = (bf16[2048,2,256]{2,1,0:T(2,128)(2,1)S(1)}, bf16[2048,2,256]{2,1,0:T(2,128)(2,1)}, u32[]{:S(2)}) copy-start(bf16[2048,2,256]{2,1,0:T(2,128)(2,1)} %param.12) | copy-start | bytes 6291460
  20.9 94.6 %all-to-all-start = ((bf16[4,4,32,4096]{3,2,1,0:T(8,128)(2,1)}), bf16[4,4,32,4096]{3,2,1,0:T(8,128)(2,1)}, u32[]{:S(2)}, u32[]{:S(2)}) async-start(bf16[4,4,32,4096]{3,2,1,0:T(8,128)(2,1)} %bitcast.47), calls=%async_computation | async-start | bytes 8388608 | tf_op jit(solution)/shard_map/all_to_all | solution.py:412
  25.8 54.5 %reduce-scatter.2.cloned.1.call-start = ((), (), s32[]{:S(2)}) async-start(), calls=%async_computation.3 | async-start | bytes 663552 | tf_op jit(solution)/shard_map/reduce_scatter | solution.py:430
  34.9 10.7 %copy-start.2 = (s32[8]{0:T(128)S(1)}, s32[8]{0:T(128)}, u32[]{:S(2)}) copy-start(s32[8]{0:T(128)} %param.15) | copy-start | bytes 100
  115.5 303.8 %copy-start = (bf16[8,16384]{1,0:T(8,128)(2,1)S(1)}, bf16[8,16384]{1,0:T(8,128)(2,1)}, u32[]{:S(2)}) copy-start(bf16[8,16384]{1,0:T(8,128)(2,1)} %param.9) | copy-start | bytes 786436
Sparse Core Ops, SparseCore 0:
  44.7 35.5 reduce-scatter.1

commit v4 on v3

--- a/solution.py
+++ b/solution.py
@@ -66,16 +66,15 @@
     tensor_count,
     send_index,
     source,
-    early,
     partial,
-    incoming,
-    attention,
-    *scratch,
+    *refs,
 ):
+    early = refs[: tensor_count - 1]
+    incoming, attention, *scratch = refs[tensor_count - 1 :]
     blocks, block_rows, _ = source.shape
     columns = incoming.shape[2]
     capacity = incoming.shape[0] // dp_count
-    parts, early_chunks = chunk_list(block_rows, early.shape[1], columns)
+    parts, early_chunks = chunk_list(block_rows, early[0].shape[1], columns)
     chunks = len(parts)
     held = scratch[:chunks]
     ordered = scratch[chunks : 2 * chunks]
@@ -118,16 +117,19 @@
             pl.ds(pl.multiple_of(owner * columns + column, 128), width),
         ]
 
-    def early_copy(chunk):
+    def early_copy(chunk, step):
+        owner = lax.rem(mine + tensor_count - step, tensor_count)
         return pltpu.make_async_copy(
-            early.at[:, pl.ds(parts[chunk][0], CHUNK), :], held[chunk], early_sem.at[chunk]
+            early[step - 1].at[:, pl.ds(parts[chunk][0], CHUNK), :],
+            held[chunk].at[pl.ds(owner * blocks, blocks)],
+            early_sem.at[chunk, step],
         )
 
     def own_copy(chunk):
         return pltpu.make_async_copy(
             tile(chunk, mine),
             held[chunk].at[pl.ds(mine * blocks, blocks)],
-            own_sem.at[chunk - early_chunks],
+            own_sem.at[chunk],
         )
 
     def tensor_copy(chunk, step):
@@ -233,7 +235,9 @@
     for chunk in range(early_chunks, min(early_chunks + AHEAD, chunks)):
         start_tensor(chunk)
     for chunk in range(early_chunks):
-        early_copy(chunk).start()
+        own_copy(chunk).start()
+        for step in range(1, tensor_count):
+            early_copy(chunk, step).start()
     att_own = pltpu.make_async_copy(partial.at[me], gathered.at[me], att_sem)
     share_own = pltpu.make_async_copy(total, attention.at[mine], share_sem)
     att_own.start()
@@ -245,7 +249,9 @@
         if chunk == early_chunks + AHEAD:
             start_share()
         if chunk < early_chunks:
-            early_copy(chunk).wait()
+            own_copy(chunk).wait()
+            for step in range(1, tensor_count):
+                early_copy(chunk, step).wait()
         else:
             own_copy(chunk).wait()
             for step in range(1, tensor_count):
@@ -279,7 +285,7 @@
     blocks, block_rows, width = source.shape
     group_size = blocks * tensor_count
     columns = width // tensor_count
-    parts, early_chunks = chunk_list(block_rows, early.shape[1], columns)
+    parts, early_chunks = chunk_list(block_rows, early[0].shape[1], columns)
     chunks = len(parts)
     late = chunks - early_chunks
     slots = dp_count * capacity
@@ -293,7 +299,7 @@
             jax.ShapeDtypeStruct((slots, block_rows, columns), jnp.bfloat16),
             jax.ShapeDtypeStruct(exchanged, jnp.bfloat16),
         ),
-        in_specs=[pl.BlockSpec(memory_space=pltpu.SMEM), anywhere, anywhere, anywhere],
+        in_specs=[pl.BlockSpec(memory_space=pltpu.SMEM)] + [anywhere] * (1 + tensor_count),
         out_specs=(anywhere, anywhere),
         scratch_shapes=[
             pltpu.VMEM((group_size, CHUNK, part[2]), jnp.bfloat16) for part in parts
@@ -304,8 +310,8 @@
             pltpu.VMEM(exchanged, jnp.bfloat16),
             pltpu.VMEM(exchanged, jnp.bfloat16),
             pltpu.VMEM(shared, jnp.bfloat16),
-            dma((early_chunks,)),
-            dma((late,)),
+            dma((early_chunks, tensor_count)),
+            dma((chunks,)),
             dma((late, tensor_count)),
             dma((late, tensor_count)),
             dma((chunks,)),
@@ -327,7 +333,7 @@
             flops=0, bytes_accessed=4 * slots * block_rows * columns, transcendentals=0
         ),
         name="route",
-    )(send_index, source, early, partial)
+    )(send_index, source, partial, *early)
 
 
 def put_kernel(slot_of, incoming, out, held, read_sem, write_sem):
@@ -409,15 +415,20 @@
     dp_count = lax.axis_size("dp")
     tensor_count = lax.axis_size("tensor")
     blocks, _, width = next_source.shape
-    early = lax.all_to_all(
-        next_source[:, :EARLY]
-        .reshape(blocks, EARLY, tensor_count, width // tensor_count)
-        .transpose(2, 0, 1, 3),
-        "tensor",
-        split_axis=0,
-        concat_axis=0,
-        tiled=True,
-    ).reshape(tensor_count * blocks, EARLY, width // tensor_count)
+    columns = width // tensor_count
+    mine = lax.axis_index("tensor")
+    early = [
+        lax.ppermute(
+            lax.dynamic_slice(
+                next_source,
+                (0, 0, lax.rem(mine + step, tensor_count) * columns),
+                (blocks, EARLY, columns),
+            ),
+            "tensor",
+            [(place, (place + step) % tensor_count) for place in range(tensor_count)],
+        )
+        for step in range(1, tensor_count)
+    ]
     send_index, slot_of, capacity = routing_tables(block_ids, dp_count)
     stream = hidden.astype(jnp.float32)
     meansq = jnp.mean(stream * stream, axis=-1, keepdims=True)

time: 440 us -> 437 us (level)
  waiting for transfers between devices: 42.8 us -> 33.5 us
    all_to_all x1 -> x0, waiting for transfers between devices: 7.06 us -> none  [on_device(): lax.all_to_all(next_source[:, :EARLY].reshape(blocks, EARLY, tensor_count...]
    all_to_all x1 -> x0, starting transfers between devices: 4.84 us -> none  [on_device(): lax.all_to_all(next_source[:, :EARLY].reshape(blocks, EARLY, tensor_count...]
  transfers between devices with their start and end apart: 3 -> 5, of which waited for: 3 -> 1; matrix products, arithmetic and copies ran while one was open for 7% -> 9% of each run, Pallas kernels for 0% -> 0%
where the time goes in v4:
time: 437 us; the launch traced here: 435 us
  Pallas kernels  319 us (73%)
  waiting for transfers between devices  33.5 us (8%)
  matrix products  24.8 us (6%)
  blocking collectives  18 us (4%)
  between operations  14.9 us (3%)
  local copies, waits for them, and re-layouts  10.8 us (2%)
  starting transfers between devices  7.68 us (2%)
  other arithmetic  7.02 us (2%)
    pallas_call x1, Pallas kernels, route(): pl.pallas_call(functools.partial(route_kernel, dp_count, tensor_count), o...  306 us
    reduce_scatter x1, waiting for transfers between devices, on_device(): lax.psum_scatter(jnp.concatenate([jnp.dot(pieces, query_weight, preferred...  33.5 us
    pallas_call x1, Pallas kernels, put(): pl.pallas_call(put_kernel, out_shape=jax.ShapeDtypeStruct(shape, jnp.bflo...  12.6 us
    all_gather x1, blocking collectives, on_device(): lax.all_gather(heads_out, 'dp', axis=0, tiled=True)  10.6 us
    dot_general x1, matrix products, on_device(): jnp.dot(pieces, query_weight, preferred_element_type=jnp.float32)  8.94 us
    dot_general x1, matrix products, on_device(): jnp.dot(lax.all_gather(heads_out, 'dp', axis=0, tiled=True), output_weigh...  8.81 us
  transfers between devices with their start and end apart: 5, of which 1 were waited for; matrix products, arithmetic and copies ran while one was open for 9% of the time, Pallas kernels for 0%

profile of v4, /device:TPU:25, one launch (start us, length us, event | category | flops | bytes accessed | tf_op | source)
XLA Modules:
  0.0 435.4 jit_solution(5797695054916938358)
XLA Ops:
  7.2 1.2 fusion.17
  8.4 0.8 convert_element_type.49
  9.1 1.8 fusion.19
  10.9 4.4 %all-to-all-start = ((bf16[8,8,2048]{2,0,1:T(8,128)(2,1)}), bf16[8,8,2048]{2,0,1:T(8,128)(2,1)S(1)}, u32[]{:S(2)}, u32[]{:S(2)}) async-start(bf16[8,8,2048]{2,0,1:T(8,128)(2,1)} %bitcast.2), calls=%async_computation | async-start | bytes 524288 | tf_op jit(solution)/shard_map/all_to_all | solution.py:438
  15.3 3.6 constant_dynamic-slice_fusion
  19.2 3.0 collective-permute-start
  22.2 1.2 dynamic-slice
  24.1 0.9 dynamic-update-slice
  25.0 7.4 %all-reduce = s32[128]{0:T(128)S(1)} all-reduce(s32[128]{0:T(128)S(1)} %dynamic-update-slice), channel_id=2, replica_groups=mesh['dp'=8,'tensor'=4] {'dp'}, use_global_device_ids=true, to_apply=%add | all-reduce | flops 128 | bytes 1024
  32.5 3.4 copy.17
  36.2 8.9 %convolution_convert_fusion = bf16[64,4096]{1,0:T(8,128)(2,1)S(1)} fusion(bf16[2048,4096]{1,0:T(8,128)(2,1)} %param.11, bf16[8,8,2048]{2,0,1:T(8,128)(2,1)S(1)} %all-to-all-done), kind=kOutput, calls=%fused_computation | convolution fusion | flops 1074003968 | bytes 17563648 | tf_op jit(solution)/shard_map/dot_general | solution.py:444
  45.1 0.5 convolution_convert_fusion.1
  45.6 0.9 pad_maximum_fusion
  46.8 0.7 select_reduce_fusion.slot_of
  47.6 33.5 %reduce-scatter.2.cloned.1.call-done = bf16[8,4608]{1,0:T(8,128)(2,1)} async-done(((bf16[64,4608]{1,0:T(8,128)(2,1)}), bf16[8,4608]{1,0:T(8,128)(2,1)}) %reduce-scatter.2.cloned.1.call-update) | async-done | bytes 73744 | tf_op jit(solution)/shard_map/reduce_scatter | solution.py:441
  81.1 0.7 slice.27
  81.8 0.8 slice.26
  82.8 3.5 fusion.34
  86.6 3.0 fusion.13
  89.6 10.6 %all_gather.11 = bf16[64,4096]{1,0:T(8,128)(2,1)S(1)} all-gather(bf16[8,4096]{1,0:T(8,128)(2,1)S(1)} %bitcast.41), channel_id=1, replica_groups=mesh['dp'=8,'tensor'=4] {'dp'}, dimensions={0}, use_global_device_ids=true | all-gather | bytes 589824 | tf_op jit(solution)/shard_map/all_gather | solution.py:461
  100.3 8.8 %convolution_bitcast_fusion.partial = f32[8,8,2048]{2,1,0:T(8,128)S(1)} fusion(bf16[64,4096]{1,0:T(8,128)(2,1)S(1)} %all_gather.11, bf16[4096,2048]{1,0:T(8,128)(2,1)} %param.13), kind=kOutput, calls=%fused_computation.5 | convolution fusion | flops 1073741824 | bytes 17825792 | tf_op jit(solution)/shard_map/dot_general | solution.py:460
  109.1 305.9 %route.1 = (bf16[16,128,4096]{2,1,0:T(8,128)(2,1)}, bf16[4,16,2048]{2,1,0:T(8,128)(2,1)S(1)}) custom-call(s32[16]{0:T(128)S(1)} %select_reduce_fusion.1.send_index, bf16[4,128,16384]{2,1,0:T(8,128)(2,1)} %source.1, f32[8,8,2048]{2,1,0:T(8,128)S(1)} %convolution_bitcast_fusion.partial, bf16[4,32,4096]{2,1,0:T(8,128)(2,1)S(1)} %collective-permute-done.refs_0_, ...), custom_call_target="tpu_custom_call" | custom-call | bytes 33554432 | tf_op jit(solution)/shard_map/route/pallas_call | solution.py:296
  415.1 0.7 fusion.20
  415.9 12.6 %put.1 = bf16[16,128,4096]{2,1,0:T(8,128)(2,1)} custom-call(s32[16]{0:T(128)} %select_reduce_fusion.slot_of, bf16[16,128,4096]{2,1,0:T(8,128)(2,1)} %get-tuple-element.5.incoming), custom_call_target="tpu_custom_call" | custom-call | tf_op jit(solution)/shard_map/put/pallas_call | solution.py:362
  (35 shorter events, 1.6 us)
Async XLA Ops:
  10.9 25.2 %all-to-all-start = ((bf16[8,8,2048]{2,0,1:T(8,128)(2,1)}), bf16[8,8,2048]{2,0,1:T(8,128)(2,1)S(1)}, u32[]{:S(2)}, u32[]{:S(2)}) async-start(bf16[8,8,2048]{2,0,1:T(8,128)(2,1)} %bitcast.2), calls=%async_computation | async-start | bytes 524288 | tf_op jit(solution)/shard_map/all_to_all | solution.py:438
  15.3 65.8 %reduce-scatter.2.cloned.1.call-start = ((), (), s32[]{:S(2)}) async-start(), calls=%async_computation.2 | async-start | bytes 663552 | tf_op jit(solution)/shard_map/reduce_scatter | solution.py:441
  18.9 90.2 %collective-permute-start.2 = (bf16[4,32,4096]{2,1,0:T(8,128)(2,1)}, bf16[4,32,4096]{2,1,0:T(8,128)(2,1)S(1)}, u32[]{:S(2)}, u32[]{:S(2)}) collective-permute-start(bf16[4,32,4096]{2,1,0:T(8,128)(2,1)} %get-tuple-element.6), channel_id=1, source_target_pairs={{0,3},{1,0},{2,1},{3,2},{4,7},{5,4},{6,5},{7,6},{8,11},{9,8},{10,9... | collective-permute-start | bytes 3145736 | tf_op jit(solution)/shard_map/ppermute | solution.py:421
  19.1 90.0 %collective-permute-start.1 = (bf16[4,32,4096]{2,1,0:T(8,128)(2,1)}, bf16[4,32,4096]{2,1,0:T(8,128)(2,1)S(1)}, u32[]{:S(2)}, u32[]{:S(2)}) collective-permute-start(bf16[4,32,4096]{2,1,0:T(8,128)(2,1)} %get-tuple-element.7), channel_id=1, source_target_pairs={{0,2},{1,3},{2,0},{3,1},{4,6},{5,7},{6,4},{7,5},{8,10},{9,11},{10,... | collective-permute-start | bytes 3145736 | tf_op jit(solution)/shard_map/ppermute | solution.py:421
  19.2 89.9 %collective-permute-start = (bf16[4,32,4096]{2,1,0:T(8,128)(2,1)}, bf16[4,32,4096]{2,1,0:T(8,128)(2,1)S(1)}, u32[]{:S(2)}, u32[]{:S(2)}) collective-permute-start(bf16[4,32,4096]{2,1,0:T(8,128)(2,1)} %get-tuple-element.8), channel_id=1, source_target_pairs={{0,1},{1,2},{2,3},{3,0},{4,5},{5,6},{6,7},{7,4},{8,9},{9,10},{10,1... | collective-permute-start | bytes 3145736 | tf_op jit(solution)/shard_map/ppermute | solution.py:421
  36.1 11.3 %copy-start.2 = (s32[8]{0:T(128)S(1)}, s32[8]{0:T(128)}, u32[]{:S(2)}) copy-start(s32[8]{0:T(128)} %param.15) | copy-start | bytes 100
  36.2 9.0 %copy-start = (bf16[256,8,2,256]{3,1,2,0:T(8,128)(2,1)S(1)}, bf16[256,8,2,256]{3,1,2,0:T(8,128)(2,1)}, u32[]{:S(2)}) copy-start(bf16[256,8,2,256]{3,1,2,0:T(8,128)(2,1)} %copy.17) | copy-start | bytes 6291460
  109.1 306.0 %copy-start.1 = (bf16[8,16384]{1,0:T(8,128)(2,1)S(1)}, bf16[8,16384]{1,0:T(8,128)(2,1)}, u32[]{:S(2)}) copy-start(bf16[8,16384]{1,0:T(8,128)(2,1)} %param.9) | copy-start | bytes 786436
Sparse Core Ops, SparseCore 0:
  46.6 34.4 reduce-scatter.1
